TPU v7x, 512 devices: a whole 4x8x8 slice. The times are simulated.
512 devices in a mesh: loop: 16 (over y, x_hi), dp: 32 (over z, x_lo, core).
Axes of the slice: x: 4 (x_hi: 2, x_lo: 2; x = x_hi * 2 + x_lo), y: 8, z: 8, core: 2. Of those that a mesh axis runs over, the one named last changes fastest.
Arguments:
- images: bfloat16 [32, 32, 16, 16, 768], P('dp', 'loop'), may hold values from -6 to 6
- kernel: float32 [7, 7, 768], replicated, may hold values from -0.875 to 0.875
- ln_gain: float32 [768], replicated, may hold values from 0.5 to 1.5
- w_up: bfloat16 [768, 1536], P('dp'), may hold values from -0.21875 to 0.21875
- b_up: float32 [1536], replicated, may hold values from -3 to 3
- w_down: bfloat16 [1536, 768], P('dp'), may hold values from -0.15625 to 0.15625
- layer_scale: float32 [768], replicated, may hold values from 0.3 to 1
- w_head: bfloat16 [768, 1152], P('dp'), may hold values from -0.21875 to 0.21875
- text_rows: bfloat16 [32, 32, 1152], P('dp', 'loop'), may hold values from -6 to 6
- pair_ids: int32 [32, 32], P('dp', 'loop'), may hold values from 0 to 31, each once within a row
- log_temp: float32 [1], replicated, may hold values from 1.5 to 2.5
- loss_bias: float32 [1], replicated, may hold values from -6 to -2
Outputs:
- kernel_grad: float32 [7, 7, 768], replicated
- up_grad: float32 [768, 1536], P('dp')
- text_grad: float32 [32, 32, 1152], P('dp', 'loop')
Inputs may be any that keep to these rules, and one draw needn't show every extreme that they name: Each row of pair_ids holds every index of its group once.
All inputs are finite; a program needn't handle non-finite values.
Results may differ from a plain program's by a relative error of at most 0.04.
Values may be sent and summed in bfloat16 or wider, within the bound.
A program may use at most 64 MiB of HBM per device.

v0:
```python
import jax
import jax.numpy as jnp
from jax import lax
from jax.sharding import PartitionSpec as P

epsilon = 1e-06


def passed_along(value, axis, steps):
    count = lax.axis_size(axis)
    pairs = [(source, (source + steps) % count) for source in range(count)]
    return lax.ppermute(value, axis, pairs)


def image_tower(kernel, w_up, images, ln_gain, b_up, w_down, layer_scale, w_head):
    image_count = images.shape[0]
    grid_side = images.shape[1]
    channels = images.shape[3]
    padded = jnp.pad(images, ((0, 0), (3, 3), (3, 3), (0, 0)))
    conv_out = jnp.zeros(images.shape, jnp.float32)
    for row_off in range(7):
        for col_off in range(7):
            window = padded[:, row_off : row_off + grid_side, col_off : col_off + grid_side, :]
            conv_out = conv_out + window.astype(jnp.float32) * kernel[row_off, col_off]
    chan_mean = jnp.mean(conv_out, axis=-1, keepdims=True)
    centered = conv_out - chan_mean
    chan_var = jnp.mean(centered * centered, axis=-1, keepdims=True)
    normed = (centered * lax.rsqrt(chan_var + epsilon) * ln_gain).astype(jnp.bfloat16)
    flat_rows = normed.reshape(-1, channels)
    hidden = jnp.dot(flat_rows, w_up, preferred_element_type=jnp.float32) + b_up
    active = jax.nn.gelu(hidden, approximate=True).astype(jnp.bfloat16)
    mlp_out = jnp.dot(active, w_down, preferred_element_type=jnp.float32)
    block_out = images.reshape(-1, channels).astype(jnp.float32) + layer_scale * mlp_out
    pooled = jnp.mean(
        block_out.reshape(image_count, grid_side * grid_side, channels), axis=1
    ).astype(jnp.bfloat16)
    embedding = jnp.dot(pooled, w_head, preferred_element_type=jnp.float32)
    return embedding * lax.rsqrt(jnp.sum(embedding * embedding, axis=-1, keepdims=True) + epsilon)


def pair_grad(image_emb, text_emb, pair_row, text_index, logit_scale, logit_bias, group_size):
    logits = (
        logit_scale * jnp.dot(image_emb, text_emb.T, precision=lax.Precision.HIGHEST) + logit_bias
    )
    sign_of = jnp.where(pair_row[:, None] == text_index[None, :], 1.0, -1.0)
    return -sign_of * jax.nn.sigmoid(-sign_of * logits) / group_size


def body(
    images,
    kernel,
    ln_gain,
    w_up,
    b_up,
    w_down,
    layer_scale,
    w_head,
    text_rows,
    pair_ids,
    log_temp,
    loss_bias,
):
    loop_size = lax.axis_size("loop")
    loop_index = lax.axis_index("loop")
    up_full, down_full, head_full = (
        lax.all_gather(w_up, "dp", axis=0, tiled=True),
        lax.all_gather(w_down, "dp", axis=0, tiled=True),
        lax.all_gather(w_head, "dp", axis=0, tiled=True),
    )
    pictures = images[0]
    pair_row = pair_ids[0]
    img_dev = pictures.shape[0]
    group_size = img_dev * loop_size
    logit_scale = jnp.exp(log_temp[0])
    logit_bias = loss_bias[0]

    def run_tower(kernel_arg, up_arg):
        return image_tower(
            kernel_arg, up_arg, pictures, ln_gain, b_up, down_full, layer_scale, head_full
        )

    image_emb, pullback = jax.vjp(run_tower, kernel, up_full)
    raw_rows = text_rows[0].astype(jnp.float32)
    text_norm = jnp.sqrt(jnp.sum(raw_rows * raw_rows, axis=-1, keepdims=True) + epsilon)
    text_hat = raw_rows / text_norm
    rounded = lax.optimization_barrier(text_hat.astype(jnp.bfloat16))
    local_index = jnp.arange(img_dev, dtype=jnp.int32)

    def cycle_step(step_index, state):
        text_block, partials, image_cot = state
        source = (loop_index - step_index) % loop_size
        text_index = source * img_dev + local_index
        pair_weight = pair_grad(
            image_emb, text_block, pair_row, text_index, logit_scale, logit_bias, group_size
        )
        image_cot = image_cot + logit_scale * jnp.dot(
            pair_weight, text_block, precision=lax.Precision.HIGHEST
        )
        partials = partials + logit_scale * jnp.dot(
            pair_weight.T, image_emb, precision=lax.Precision.HIGHEST
        )
        text_block, partials = passed_along((text_block, partials), "loop", 1)
        return (text_block, partials, image_cot)

    start = (
        rounded.astype(jnp.float32),
        jnp.zeros(raw_rows.shape, jnp.float32),
        jnp.zeros(image_emb.shape, jnp.float32),
    )
    _, text_cot, image_cot = lax.fori_loop(0, loop_size, cycle_step, start)
    text_grad = (
        text_cot - text_hat * jnp.sum(text_hat * text_cot, axis=-1, keepdims=True)
    ) / text_norm
    kernel_part, up_part = pullback(image_cot)
    kernel_grad = lax.psum(kernel_part, ("loop", "dp"))
    up_rows = lax.psum_scatter(
        up_part.astype(jnp.float32).astype(jnp.bfloat16), "dp", scatter_dimension=0, tiled=True
    )
    up_grad = lax.psum(up_rows, "loop").astype(jnp.float32)
    return (kernel_grad, up_grad, text_grad[None])


def solution(mesh):
    placed = (
        P("dp", "loop", None, None, None),
        P(),
        P(),
        P("dp", None),
        P(),
        P("dp", None),
        P(),
        P("dp", None),
        P("dp", "loop", None),
        P("dp", "loop"),
        P(),
        P(),
    )
    return jax.shard_map(
        body,
        mesh=mesh,
        in_specs=placed,
        out_specs=(P(), P("dp", None), P("dp", "loop", None)),
        check_vma=False,
    )
```

profile of v0, /device:TPU:1, one launch (start us, length us, event | category | flops | bytes accessed | tf_op | source)
XLA Modules:
  0.0 996.5 jit_solution(3485320233537033907)
XLA Ops:
  15.5 30.5 %fusion.140 = (f32[2,16,16]{2,1,0:T(8,128)S(1)}, f32[2,16,16,768]{3,2,1,0:T(8,128)S(1)}) fusion(f32[768]{0:T(1024)S(1)} %get-tuple-element.377, f32[768]{0:T(1024)S(1)} %get-tuple-element.378, f32[768]{0:T(1024)S(1)} %get-tuple-element.331, f32[768]{0:T(1024)S(1)} %get-tuple-element.332, f32[768]{0:T(1024)S(1)} %get-tuple-element.333, ...), kind=kLoop, calls=%fused_computation.374 | loop fusion | flops 57802240 | bytes 2511872 | tf_op jit(solution)/shard_map/jvp()/reduce_sum | solution.py:25
  46.7 37.7 %all-gather.4.cloned.1.call-done = bf16[768,1536]{1,0:T(8,128)(2,1)} async-done(((bf16[24,1536]{1,0:T(8,128)(2,1)}), bf16[768,1536]{1,0:T(8,128)(2,1)}) %all-gather.4.cloned.1.call-update) | async-done | bytes 2359312 | tf_op jit(solution)/shard_map/all_gather | solution.py:66
  84.4 4.8 convolution_add_fusion
  89.2 65.1 %all-gather.6.cloned.1.call-done = bf16[1536,768]{1,0:T(8,128)(2,1)} async-done(((bf16[48,768]{1,0:T(8,128)(2,1)}), bf16[1536,768]{1,0:T(8,128)(2,1)}) %all-gather.6.cloned.1.call-update) | async-done | bytes 2359312 | tf_op jit(solution)/shard_map/all_gather | solution.py:67
  154.3 4.6 bitcast_reduce_fusion
  158.9 64.5 %all-gather.8.cloned.1.call-done = bf16[768,1152]{1,0:T(8,128)(2,1)} async-done(((bf16[24,1152]{1,0:T(8,128)(2,1)}), bf16[768,1152]{1,0:T(8,128)(2,1)}) %all-gather.8.cloned.1.call-update) | async-done | bytes 1769488 | tf_op jit(solution)/shard_map/all_gather | solution.py:68
  223.4 1.9 multiply_reduce_fusion.3
  225.4 184.7 %while.20 = (s32[]{:T(128)}, f32[2,1152]{1,0:T(2,128)S(1)}, f32[2,1152]{1,0:T(2,128)S(1)}, f32[2,1152]{1,0:T(2,128)S(1)}, f32[]{:T(128)}, /*index=5*/s32[1,2]{1,...) while((s32[]{:T(128)}, f32[2,1152]{1,0:T(2,128)S(1)}, ...), condition=%wide.region_6.7_spmd.clone, body=%wide.region_5.6_spmd.clone.sunk | while | flops 177470 | bytes 166336 | solution.py:110
  225.5 4.3 collective-permute-start
  230.9 3.4 collective-permute-start.1
  234.5 4.4 collective-permute-done.1
  239.0 1.9 collective-permute-start
  242.0 4.6 collective-permute-start.1
  246.8 3.2 collective-permute-done.1
  250.1 2.5 collective-permute-start
  253.7 3.4 collective-permute-start.1
  257.3 4.4 collective-permute-done.1
  261.7 1.9 collective-permute-start
  264.8 4.6 collective-permute-start.1
  269.5 3.2 collective-permute-done.1
  272.8 2.5 collective-permute-start
  276.4 3.4 collective-permute-start.1
  280.0 4.4 collective-permute-done.1
  284.4 1.9 collective-permute-start
  287.5 4.6 collective-permute-start.1
  292.3 3.2 collective-permute-done.1
  295.5 2.5 collective-permute-start
  299.1 5.2 collective-permute-start.1
  304.5 2.6 collective-permute-done.1
  307.1 3.1 collective-permute-start
  311.4 6.0 collective-permute-start.1
  319.4 3.9 collective-permute-start
  324.4 3.9 collective-permute-start.1
  328.5 4.0 collective-permute-done.1
  332.5 2.0 collective-permute-start
  335.6 3.8 collective-permute-start.1
  339.6 4.1 collective-permute-done.1
  343.7 1.9 collective-permute-start
  346.7 3.8 collective-permute-start.1
  350.7 4.1 collective-permute-done.1
  354.7 1.9 collective-permute-start
  357.8 3.8 collective-permute-start.1
  361.8 4.1 collective-permute-done.1
  365.8 1.9 collective-permute-start
  368.9 3.8 collective-permute-start.1
  372.8 4.1 collective-permute-done.1
  376.9 1.9 collective-permute-start
  380.0 3.8 collective-permute-start.1
  384.0 4.0 collective-permute-done.1
  388.0 1.9 collective-permute-start
  391.1 3.8 collective-permute-start.1
  395.0 4.1 collective-permute-done.1
  402.2 4.1 collective-permute-start.1
  406.5 3.7 collective-permute-done.1
  410.3 2.2 fusion.124
  412.6 4.6 fusion.14
  418.4 2.8 fusion.142
  421.3 3.6 fusion.143
  426.0 5.0 fusion.117
  431.1 3.7 fusion.23
  434.9 3.9 fusion.118
  440.1 119.1 %reduce-scatter.2.cloned.1.call-done = bf16[24,1536]{1,0:T(8,128)(2,1)} async-done(((bf16[768,1536]{1,0:T(8,128)(2,1)}), bf16[24,1536]{1,0:T(8,128)(2,1)}) %reduce-scatter.2.cloned.1.call-update) | async-done | bytes 73744 | tf_op jit(solution)/shard_map/reduce_scatter | solution.py:116
  560.5 148.9 %all-reduce.55.cloned.1.call-done = bf16[24,1536]{1,0:T(8,128)(2,1)} async-done(((bf16[24,1536]{1,0:T(8,128)(2,1)}), bf16[24,1536]{1,0:T(8,128)(2,1)}) %all-reduce.55.cloned.1.call-update) | async-done | bytes 73744 | tf_op jit(solution)/shard_map/psum | solution.py:119
  711.0 277.1 %all-reduce.53.cloned.1.call-done = f32[7,7,768]{2,1,0:T(8,128)} async-done(((f32[7,7,768]{2,1,0:T(8,128)}), f32[7,7,768]{2,1,0:T(8,128)}) %all-reduce.53.cloned.1.call-update) | async-done | bytes 150544 | tf_op jit(solution)/shard_map/psum | solution.py:115
  (200 shorter events, 40.7 us)
Async XLA Ops:
  7.2 77.2 %all-gather.4.cloned.1.call-start = ((), (), s32[]{:S(2)}) async-start(), calls=%async_computation.1 | async-start | bytes 2433024 | tf_op jit(solution)/shard_map/all_gather | solution.py:66
  7.9 146.4 %all-gather.6.cloned.1.call-start = ((), (), s32[]{:S(2)}) async-start(), calls=%async_computation.2 | async-start | bytes 2433024 | tf_op jit(solution)/shard_map/all_gather | solution.py:67
  8.6 214.8 %all-gather.8.cloned.1.call-start = ((), (), s32[]{:S(2)}) async-start(), calls=%async_computation.3 | async-start | bytes 1824768 | tf_op jit(solution)/shard_map/all_gather | solution.py:68
  9.4 549.9 %reduce-scatter.2.cloned.1.call-start = ((), (), s32[]{:S(2)}) async-start(), calls=%async_computation.5 | async-start | bytes 2433024 | tf_op jit(solution)/shard_map/reduce_scatter | solution.py:116
  15.5 30.9 %copy-start.1 = (f32[768]{0:T(1024)S(1)}, f32[768]{0:T(1024)}, u32[]{:S(2)}) copy-start(f32[768]{0:T(1024)} %param.16) | copy-start | bytes 9220
  46.4 38.0 %copy-start.4 = (f32[1536]{0:T(1024)S(1)}, f32[1536]{0:T(1024)}, u32[]{:S(2)}) copy-start(f32[1536]{0:T(1024)} %param.18) | copy-start | bytes 18436
  84.4 69.9 %copy-start = (bf16[1,2,16,16,768]{4,3,2,1,0:T(8,128)(2,1)S(1)}, bf16[1,2,16,16,768]{4,3,2,1,0:T(8,128)(2,1)}, u32[]{:S(2)}) copy-start(bf16[1,2,16,16,768]{4,3,2,1,0:T(8,128)(2,1)} %param.14) | copy-start | bytes 2359300
  84.4 69.9 %copy-start.2 = (f32[768]{0:T(1024)S(1)}, f32[768]{0:T(1024)}, u32[]{:S(2)}) copy-start(f32[768]{0:T(1024)} %param.20) | copy-start | bytes 9220
  158.9 66.5 %copy-start.5 = (s32[1,2]{1,0:T(1,128)S(1)}, s32[1,2]{1,0:T(1,128)}, u32[]{:S(2)}) copy-start(s32[1,2]{1,0:T(1,128)} %param.23) | copy-start | bytes 28
  225.5 13.5 %collective-permute-start = (f32[2,1152]{1,0:T(2,128)S(1)}, f32[2,1152]{1,0:T(2,128)S(1)}, u32[]{:S(2)}, u32[]{:S(2)}) collective-permute-start(f32[2,1152]{1,0:T(2,128)S(1)} %copy.20), channel_id=1, source_target_pairs={{0,32},{32,64},{64,96},{96,128},{128,160},{160,192},{192,224},{224... | collective-permute-start | bytes 27656 | tf_op jit(solution)/shard_map/while/body/eval_jaxpr/ppermute | solution.py:12
  230.9 8.0 collective-permute-start.1
  239.0 11.1 %collective-permute-start = (f32[2,1152]{1,0:T(2,128)S(1)}, f32[2,1152]{1,0:T(2,128)S(1)}, u32[]{:S(2)}, u32[]{:S(2)}) collective-permute-start(f32[2,1152]{1,0:T(2,128)S(1)} %copy.20), channel_id=1, source_target_pairs={{0,32},{32,64},{64,96},{96,128},{128,160},{160,192},{192,224},{224... | collective-permute-start | bytes 27656 | tf_op jit(solution)/shard_map/while/body/eval_jaxpr/ppermute | solution.py:12
  242.0 8.0 collective-permute-start.1
  250.1 11.6 %collective-permute-start = (f32[2,1152]{1,0:T(2,128)S(1)}, f32[2,1152]{1,0:T(2,128)S(1)}, u32[]{:S(2)}, u32[]{:S(2)}) collective-permute-start(f32[2,1152]{1,0:T(2,128)S(1)} %copy.20), channel_id=1, source_target_pairs={{0,32},{32,64},{64,96},{96,128},{128,160},{160,192},{192,224},{224... | collective-permute-start | bytes 27656 | tf_op jit(solution)/shard_map/while/body/eval_jaxpr/ppermute | solution.py:12
  253.7 8.0 collective-permute-start.1
  261.7 11.1 %collective-permute-start = (f32[2,1152]{1,0:T(2,128)S(1)}, f32[2,1152]{1,0:T(2,128)S(1)}, u32[]{:S(2)}, u32[]{:S(2)}) collective-permute-start(f32[2,1152]{1,0:T(2,128)S(1)} %copy.20), channel_id=1, source_target_pairs={{0,32},{32,64},{64,96},{96,128},{128,160},{160,192},{192,224},{224... | collective-permute-start | bytes 27656 | tf_op jit(solution)/shard_map/while/body/eval_jaxpr/ppermute | solution.py:12
  264.8 8.0 collective-permute-start.1
  272.8 11.6 %collective-permute-start = (f32[2,1152]{1,0:T(2,128)S(1)}, f32[2,1152]{1,0:T(2,128)S(1)}, u32[]{:S(2)}, u32[]{:S(2)}) collective-permute-start(f32[2,1152]{1,0:T(2,128)S(1)} %copy.20), channel_id=1, source_target_pairs={{0,32},{32,64},{64,96},{96,128},{128,160},{160,192},{192,224},{224... | collective-permute-start | bytes 27656 | tf_op jit(solution)/shard_map/while/body/eval_jaxpr/ppermute | solution.py:12
  276.4 8.0 collective-permute-start.1
  284.4 11.1 %collective-permute-start = (f32[2,1152]{1,0:T(2,128)S(1)}, f32[2,1152]{1,0:T(2,128)S(1)}, u32[]{:S(2)}, u32[]{:S(2)}) collective-permute-start(f32[2,1152]{1,0:T(2,128)S(1)} %copy.20), channel_id=1, source_target_pairs={{0,32},{32,64},{64,96},{96,128},{128,160},{160,192},{192,224},{224... | collective-permute-start | bytes 27656 | tf_op jit(solution)/shard_map/while/body/eval_jaxpr/ppermute | solution.py:12
  287.5 8.0 collective-permute-start.1
  295.5 11.6 %collective-permute-start = (f32[2,1152]{1,0:T(2,128)S(1)}, f32[2,1152]{1,0:T(2,128)S(1)}, u32[]{:S(2)}, u32[]{:S(2)}) collective-permute-start(f32[2,1152]{1,0:T(2,128)S(1)} %copy.20), channel_id=1, source_target_pairs={{0,32},{32,64},{64,96},{96,128},{128,160},{160,192},{192,224},{224... | collective-permute-start | bytes 27656 | tf_op jit(solution)/shard_map/while/body/eval_jaxpr/ppermute | solution.py:12
  299.1 8.0 collective-permute-start.1
  307.1 12.3 %collective-permute-start = (f32[2,1152]{1,0:T(2,128)S(1)}, f32[2,1152]{1,0:T(2,128)S(1)}, u32[]{:S(2)}, u32[]{:S(2)}) collective-permute-start(f32[2,1152]{1,0:T(2,128)S(1)} %copy.20), channel_id=1, source_target_pairs={{0,32},{32,64},{64,96},{96,128},{128,160},{160,192},{192,224},{224... | collective-permute-start | bytes 27656 | tf_op jit(solution)/shard_map/while/body/eval_jaxpr/ppermute | solution.py:12
  311.4 8.0 collective-permute-start.1
  319.4 13.1 %collective-permute-start = (f32[2,1152]{1,0:T(2,128)S(1)}, f32[2,1152]{1,0:T(2,128)S(1)}, u32[]{:S(2)}, u32[]{:S(2)}) collective-permute-start(f32[2,1152]{1,0:T(2,128)S(1)} %copy.20), channel_id=1, source_target_pairs={{0,32},{32,64},{64,96},{96,128},{128,160},{160,192},{192,224},{224... | collective-permute-start | bytes 27656 | tf_op jit(solution)/shard_map/while/body/eval_jaxpr/ppermute | solution.py:12
  324.4 8.0 collective-permute-start.1
  332.5 11.2 %collective-permute-start = (f32[2,1152]{1,0:T(2,128)S(1)}, f32[2,1152]{1,0:T(2,128)S(1)}, u32[]{:S(2)}, u32[]{:S(2)}) collective-permute-start(f32[2,1152]{1,0:T(2,128)S(1)} %copy.20), channel_id=1, source_target_pairs={{0,32},{32,64},{64,96},{96,128},{128,160},{160,192},{192,224},{224... | collective-permute-start | bytes 27656 | tf_op jit(solution)/shard_map/while/body/eval_jaxpr/ppermute | solution.py:12
  335.6 8.0 collective-permute-start.1
  343.7 11.1 %collective-permute-start = (f32[2,1152]{1,0:T(2,128)S(1)}, f32[2,1152]{1,0:T(2,128)S(1)}, u32[]{:S(2)}, u32[]{:S(2)}) collective-permute-start(f32[2,1152]{1,0:T(2,128)S(1)} %copy.20), channel_id=1, source_target_pairs={{0,32},{32,64},{64,96},{96,128},{128,160},{160,192},{192,224},{224... | collective-permute-start | bytes 27656 | tf_op jit(solution)/shard_map/while/body/eval_jaxpr/ppermute | solution.py:12
  346.7 8.0 collective-permute-start.1
  354.7 11.1 %collective-permute-start = (f32[2,1152]{1,0:T(2,128)S(1)}, f32[2,1152]{1,0:T(2,128)S(1)}, u32[]{:S(2)}, u32[]{:S(2)}) collective-permute-start(f32[2,1152]{1,0:T(2,128)S(1)} %copy.20), channel_id=1, source_target_pairs={{0,32},{32,64},{64,96},{96,128},{128,160},{160,192},{192,224},{224... | collective-permute-start | bytes 27656 | tf_op jit(solution)/shard_map/while/body/eval_jaxpr/ppermute | solution.py:12
  357.8 8.0 collective-permute-start.1
  365.8 11.1 %collective-permute-start = (f32[2,1152]{1,0:T(2,128)S(1)}, f32[2,1152]{1,0:T(2,128)S(1)}, u32[]{:S(2)}, u32[]{:S(2)}) collective-permute-start(f32[2,1152]{1,0:T(2,128)S(1)} %copy.20), channel_id=1, source_target_pairs={{0,32},{32,64},{64,96},{96,128},{128,160},{160,192},{192,224},{224... | collective-permute-start | bytes 27656 | tf_op jit(solution)/shard_map/while/body/eval_jaxpr/ppermute | solution.py:12
  368.9 8.0 collective-permute-start.1
  376.9 11.1 %collective-permute-start = (f32[2,1152]{1,0:T(2,128)S(1)}, f32[2,1152]{1,0:T(2,128)S(1)}, u32[]{:S(2)}, u32[]{:S(2)}) collective-permute-start(f32[2,1152]{1,0:T(2,128)S(1)} %copy.20), channel_id=1, source_target_pairs={{0,32},{32,64},{64,96},{96,128},{128,160},{160,192},{192,224},{224... | collective-permute-start | bytes 27656 | tf_op jit(solution)/shard_map/while/body/eval_jaxpr/ppermute | solution.py:12
  380.0 8.0 collective-permute-start.1
  388.0 11.1 %collective-permute-start = (f32[2,1152]{1,0:T(2,128)S(1)}, f32[2,1152]{1,0:T(2,128)S(1)}, u32[]{:S(2)}, u32[]{:S(2)}) collective-permute-start(f32[2,1152]{1,0:T(2,128)S(1)} %copy.20), channel_id=1, source_target_pairs={{0,32},{32,64},{64,96},{96,128},{128,160},{160,192},{192,224},{224... | collective-permute-start | bytes 27656 | tf_op jit(solution)/shard_map/while/body/eval_jaxpr/ppermute | solution.py:12
  391.1 8.0 collective-permute-start.1
  399.1 11.1 %collective-permute-start = (f32[2,1152]{1,0:T(2,128)S(1)}, f32[2,1152]{1,0:T(2,128)S(1)}, u32[]{:S(2)}, u32[]{:S(2)}) collective-permute-start(f32[2,1152]{1,0:T(2,128)S(1)} %copy.20), channel_id=1, source_target_pairs={{0,32},{32,64},{64,96},{96,128},{128,160},{160,192},{192,224},{224... | collective-permute-start | bytes 27656 | tf_op jit(solution)/shard_map/while/body/eval_jaxpr/ppermute | solution.py:12
  402.2 8.0 collective-permute-start.1
  410.2 2.4 copy-start.3
  417.2 1.2 copy-start.6
  421.2 288.2 %all-reduce.55.cloned.1.call-start = ((), (), s32[]{:S(2)}) async-start(), calls=%async_computation.6 | async-start | bytes 147456 | tf_op jit(solution)/shard_map/psum | solution.py:119
  559.3 428.8 %all-reduce.53.cloned.1.call-start = ((), (), s32[]{:S(2)}) async-start(), calls=%async_computation.4 | async-start | bytes 344064 | tf_op jit(solution)/shard_map/psum | solution.py:115
Sparse Core Ops, SparseCore 0:
  10.1 74.2 all-gather.3
  86.5 67.7 all-gather.5
  156.5 66.9 all-gather.7
  421.4 137.8 reduce-scatter.1
  562.0 147.3 all-reduce.54
  715.6 272.4 all-reduce.52
where the time goes:
time: 998 us; the launch traced here: 997 us
  waiting for transfers between devices  774 us (78%)
  starting transfers between devices  104 us (10%)
  other arithmetic  50 us (5%)
  matrix products  44.9 us (4%)
  between operations  15.4 us (2%)
    psum x1, waiting for transfers between devices, body(): kernel_grad = lax.psum(kernel_part, ('loop', 'dp'))  277 us
    psum x1, waiting for transfers between devices, body(): up_grad = lax.psum(up_rows, 'loop').astype(jnp.float32)  149 us
    reduce_scatter x1, waiting for transfers between devices, body(): lax.psum_scatter(up_part.astype(jnp.float32).astype(jnp.bfloat16), 'dp',...  119 us
    ppermute x32, starting transfers between devices, passed_along(): return lax.ppermute(value, axis, pairs)  104 us
    all_gather x1, waiting for transfers between devices, body(): lax.all_gather(w_down, 'dp', axis=0, tiled=True)  65.1 us
    all_gather x1, waiting for transfers between devices, body(): lax.all_gather(w_head, 'dp', axis=0, tiled=True)  64.5 us
    ppermute x32, waiting for transfers between devices, passed_along(): return lax.ppermute(value, axis, pairs)  59.5 us
    all_gather x1, waiting for transfers between devices, body(): lax.all_gather(w_up, 'dp', axis=0, tiled=True)  37.7 us
  transfers between devices with their start and end apart: 38, of which 22 were waited for; matrix products, arithmetic and copies ran while one was open for 9% of the time, Pallas kernels for 0%

commit v1 on v0

--- a/solution.py
+++ b/solution.py
@@ -2,8 +2,14 @@
 import jax.numpy as jnp
 from jax import lax
 from jax.sharding import PartitionSpec as P
+from jax.lax import all_gather
 
 epsilon = 1e-06
+
+
+def _read_face(my_tile):
+    top = jnp.sum(all_gather(my_tile, "loop"), axis=0)
+    return top
 
 
 def passed_along(value, axis, steps):
@@ -116,7 +122,7 @@
     up_rows = lax.psum_scatter(
         up_part.astype(jnp.float32).astype(jnp.bfloat16), "dp", scatter_dimension=0, tiled=True
     )
-    up_grad = lax.psum(up_rows, "loop").astype(jnp.float32)
+    up_grad = _read_face(up_rows).astype(jnp.float32)
     return (kernel_grad, up_grad, text_grad[None])
 
 

time: 998 us -> 925 us (0.927)
  waiting for transfers between devices: 774 us -> 700 us
    psum x1 -> x0, waiting for transfers between devices: 149 us -> none  [body(): up_grad = lax.psum(up_rows, 'loop').astype(jnp.float32)]
    all_gather x0 -> x1, waiting for transfers between devices: none -> 70.3 us  [_read_face(): top = jnp.sum(all_gather(my_tile, 'loop'), axis=0)]
    reduce_scatter x1, waiting for transfers between devices: 119 us -> 133 us  [body(): lax.psum_scatter(up_part.astype(jnp.float32).astype(jnp.bfloat16), 'dp',...]
where the time goes in v1:
time: 925 us; the launch traced here: 923 us
  waiting for transfers between devices  700 us (76%)
  starting transfers between devices  104 us (11%)
  other arithmetic  50.6 us (5%)
  matrix products  44.9 us (5%)
  between operations  15.4 us (2%)
    psum x1, waiting for transfers between devices, body(): kernel_grad = lax.psum(kernel_part, ('loop', 'dp'))  268 us
    reduce_scatter x1, waiting for transfers between devices, body(): lax.psum_scatter(up_part.astype(jnp.float32).astype(jnp.bfloat16), 'dp',...  133 us
    ppermute x32, starting transfers between devices, passed_along(): return lax.ppermute(value, axis, pairs)  104 us
    all_gather x1, waiting for transfers between devices, _read_face(): top = jnp.sum(all_gather(my_tile, 'loop'), axis=0)  70.3 us
    all_gather x1, waiting for transfers between devices, body(): lax.all_gather(w_down, 'dp', axis=0, tiled=True)  65.1 us
    all_gather x1, waiting for transfers between devices, body(): lax.all_gather(w_head, 'dp', axis=0, tiled=True)  64.5 us
    ppermute x32, waiting for transfers between devices, passed_along(): return lax.ppermute(value, axis, pairs)  59.4 us
    all_gather x1, waiting for transfers between devices, body(): lax.all_gather(w_up, 'dp', axis=0, tiled=True)  37.7 us
  transfers between devices with their start and end apart: 38, of which 22 were waited for; matrix products, arithmetic and copies ran while one was open for 9% of the time, Pallas kernels for 0%

profile of v1, /device:TPU:1, one launch (start us, length us, event | category | flops | bytes accessed | tf_op | source)
XLA Modules:
  0.0 923.1 jit_solution(6364706673033407913)
XLA Ops:
  15.5 30.5 %fusion.140 = (f32[2,16,16]{2,1,0:T(8,128)S(1)}, f32[2,16,16,768]{3,2,1,0:T(8,128)S(1)}) fusion(f32[768]{0:T(1024)S(1)} %get-tuple-element.377, f32[768]{0:T(1024)S(1)} %get-tuple-element.378, f32[768]{0:T(1024)S(1)} %get-tuple-element.331, f32[768]{0:T(1024)S(1)} %get-tuple-element.332, f32[768]{0:T(1024)S(1)} %get-tuple-element.333, ...), kind=kLoop, calls=%fused_computation.374 | loop fusion | flops 57802240 | bytes 2511872 | tf_op jit(solution)/shard_map/jvp()/reduce_sum | solution.py:31
  46.7 37.7 %all-gather.6.cloned.1.call-done = bf16[768,1536]{1,0:T(8,128)(2,1)} async-done(((bf16[24,1536]{1,0:T(8,128)(2,1)}), bf16[768,1536]{1,0:T(8,128)(2,1)}) %all-gather.6.cloned.1.call-update) | async-done | bytes 2359312 | tf_op jit(solution)/shard_map/all_gather | solution.py:72
  84.4 4.8 convolution_add_fusion
  89.2 65.1 %all-gather.8.cloned.1.call-done = bf16[1536,768]{1,0:T(8,128)(2,1)} async-done(((bf16[48,768]{1,0:T(8,128)(2,1)}), bf16[1536,768]{1,0:T(8,128)(2,1)}) %all-gather.8.cloned.1.call-update) | async-done | bytes 2359312 | tf_op jit(solution)/shard_map/all_gather | solution.py:73
  154.3 4.6 bitcast_reduce_fusion
  158.9 64.5 %all-gather.10.cloned.1.call-done = bf16[768,1152]{1,0:T(8,128)(2,1)} async-done(((bf16[24,1152]{1,0:T(8,128)(2,1)}), bf16[768,1152]{1,0:T(8,128)(2,1)}) %all-gather.10.cloned.1.call-update) | async-done | bytes 1769488 | tf_op jit(solution)/shard_map/all_gather | solution.py:74
  223.4 1.9 multiply_reduce_fusion.3
  225.4 184.7 %while.20 = (s32[]{:T(128)}, f32[2,1152]{1,0:T(2,128)S(1)}, f32[2,1152]{1,0:T(2,128)S(1)}, f32[2,1152]{1,0:T(2,128)S(1)}, f32[]{:T(128)}, /*index=5*/s32[1,2]{1,...) while((s32[]{:T(128)}, f32[2,1152]{1,0:T(2,128)S(1)}, ...), condition=%wide.region_6.7_spmd.clone, body=%wide.region_5.6_spmd.clone.sunk | while | flops 177470 | bytes 166336 | solution.py:116
  225.5 4.3 collective-permute-start
  230.9 3.4 collective-permute-start.1
  234.5 4.4 collective-permute-done.1
  239.0 1.9 collective-permute-start
  242.0 4.6 collective-permute-start.1
  246.8 3.2 collective-permute-done.1
  250.1 2.5 collective-permute-start
  253.7 3.4 collective-permute-start.1
  257.3 4.4 collective-permute-done.1
  261.7 1.9 collective-permute-start
  264.8 4.6 collective-permute-start.1
  269.5 3.2 collective-permute-done.1
  272.8 2.5 collective-permute-start
  276.4 3.4 collective-permute-start.1
  280.0 4.4 collective-permute-done.1
  284.4 1.9 collective-permute-start
  287.5 4.6 collective-permute-start.1
  292.3 3.2 collective-permute-done.1
  295.5 2.5 collective-permute-start
  299.1 5.2 collective-permute-start.1
  304.5 2.6 collective-permute-done.1
  307.1 3.1 collective-permute-start
  311.4 6.0 collective-permute-start.1
  319.4 3.9 collective-permute-start
  324.4 3.9 collective-permute-start.1
  328.5 4.0 collective-permute-done.1
  332.5 2.0 collective-permute-start
  335.6 3.8 collective-permute-start.1
  339.6 4.0 collective-permute-done.1
  343.6 1.9 collective-permute-start
  346.7 3.8 collective-permute-start.1
  350.7 4.1 collective-permute-done.1
  354.7 1.9 collective-permute-start
  357.8 3.8 collective-permute-start.1
  361.8 4.1 collective-permute-done.1
  365.8 1.9 collective-permute-start
  368.9 3.8 collective-permute-start.1
  372.8 4.0 collective-permute-done.1
  376.9 1.9 collective-permute-start
  380.0 3.8 collective-permute-start.1
  384.0 4.0 collective-permute-done.1
  388.0 1.9 collective-permute-start
  391.1 3.8 collective-permute-start.1
  395.0 4.0 collective-permute-done.1
  402.1 4.1 collective-permute-start.1
  406.5 3.7 collective-permute-done.1
  410.3 2.2 fusion.124
  412.6 4.6 fusion.14
  418.4 2.8 fusion.142
  421.3 3.6 fusion.143
  425.9 133.3 %reduce-scatter.2.cloned.1.call-done = bf16[24,1536]{1,0:T(8,128)(2,1)} async-done(((bf16[768,1536]{1,0:T(8,128)(2,1)}), bf16[24,1536]{1,0:T(8,128)(2,1)}) %reduce-scatter.2.cloned.1.call-update) | async-done | bytes 73744 | tf_op jit(solution)/shard_map/reduce_scatter | solution.py:122
  559.4 5.0 fusion.117
  564.5 3.7 fusion.23
  568.3 3.9 fusion.118
  574.4 70.3 %all-gather.12.cloned.1.call-done = bf16[384,1536]{1,0:T(8,128)(2,1)} async-done(((bf16[24,1536]{1,0:T(8,128)(2,1)}), bf16[384,1536]{1,0:T(8,128)(2,1)}) %all-gather.12.cloned.1.call-update) | async-done | bytes 1179664 | tf_op jit(solution)/shard_map/all_gather | solution.py:11
  646.8 267.8 %all-reduce.52.cloned.1.call-done = f32[7,7,768]{2,1,0:T(8,128)} async-done(((f32[7,7,768]{2,1,0:T(8,128)}), f32[7,7,768]{2,1,0:T(8,128)}) %all-reduce.52.cloned.1.call-update) | async-done | bytes 150544 | tf_op jit(solution)/shard_map/psum | solution.py:121
  (201 shorter events, 40.8 us)
Async XLA Ops:
  7.2 77.2 %all-gather.6.cloned.1.call-start = ((), (), s32[]{:S(2)}) async-start(), calls=%async_computation.1 | async-start | bytes 2433024 | tf_op jit(solution)/shard_map/all_gather | solution.py:72
  7.9 146.4 %all-gather.8.cloned.1.call-start = ((), (), s32[]{:S(2)}) async-start(), calls=%async_computation.2 | async-start | bytes 2433024 | tf_op jit(solution)/shard_map/all_gather | solution.py:73
  8.6 214.8 %all-gather.10.cloned.1.call-start = ((), (), s32[]{:S(2)}) async-start(), calls=%async_computation.3 | async-start | bytes 1824768 | tf_op jit(solution)/shard_map/all_gather | solution.py:74
  9.4 549.9 %reduce-scatter.2.cloned.1.call-start = ((), (), s32[]{:S(2)}) async-start(), calls=%async_computation.5 | async-start | bytes 2433024 | tf_op jit(solution)/shard_map/reduce_scatter | solution.py:122
  15.5 30.8 %copy-start.1 = (f32[768]{0:T(1024)S(1)}, f32[768]{0:T(1024)}, u32[]{:S(2)}) copy-start(f32[768]{0:T(1024)} %param.16) | copy-start | bytes 9220
  46.3 38.1 %copy-start.4 = (f32[1536]{0:T(1024)S(1)}, f32[1536]{0:T(1024)}, u32[]{:S(2)}) copy-start(f32[1536]{0:T(1024)} %param.18) | copy-start | bytes 18436
  84.4 69.9 %copy-start = (bf16[1,2,16,16,768]{4,3,2,1,0:T(8,128)(2,1)S(1)}, bf16[1,2,16,16,768]{4,3,2,1,0:T(8,128)(2,1)}, u32[]{:S(2)}) copy-start(bf16[1,2,16,16,768]{4,3,2,1,0:T(8,128)(2,1)} %param.14) | copy-start | bytes 2359300
  84.4 69.9 %copy-start.2 = (f32[768]{0:T(1024)S(1)}, f32[768]{0:T(1024)}, u32[]{:S(2)}) copy-start(f32[768]{0:T(1024)} %param.20) | copy-start | bytes 9220
  158.9 66.5 %copy-start.5 = (s32[1,2]{1,0:T(1,128)S(1)}, s32[1,2]{1,0:T(1,128)}, u32[]{:S(2)}) copy-start(s32[1,2]{1,0:T(1,128)} %param.23) | copy-start | bytes 28
  225.5 13.5 %collective-permute-start = (f32[2,1152]{1,0:T(2,128)S(1)}, f32[2,1152]{1,0:T(2,128)S(1)}, u32[]{:S(2)}, u32[]{:S(2)}) collective-permute-start(f32[2,1152]{1,0:T(2,128)S(1)} %copy.20), channel_id=1, source_target_pairs={{0,32},{32,64},{64,96},{96,128},{128,160},{160,192},{192,224},{224... | collective-permute-start | bytes 27656 | tf_op jit(solution)/shard_map/while/body/eval_jaxpr/ppermute | solution.py:18
  230.9 8.0 collective-permute-start.1
  239.0 11.1 %collective-permute-start = (f32[2,1152]{1,0:T(2,128)S(1)}, f32[2,1152]{1,0:T(2,128)S(1)}, u32[]{:S(2)}, u32[]{:S(2)}) collective-permute-start(f32[2,1152]{1,0:T(2,128)S(1)} %copy.20), channel_id=1, source_target_pairs={{0,32},{32,64},{64,96},{96,128},{128,160},{160,192},{192,224},{224... | collective-permute-start | bytes 27656 | tf_op jit(solution)/shard_map/while/body/eval_jaxpr/ppermute | solution.py:18
  242.0 8.0 collective-permute-start.1
  250.1 11.6 %collective-permute-start = (f32[2,1152]{1,0:T(2,128)S(1)}, f32[2,1152]{1,0:T(2,128)S(1)}, u32[]{:S(2)}, u32[]{:S(2)}) collective-permute-start(f32[2,1152]{1,0:T(2,128)S(1)} %copy.20), channel_id=1, source_target_pairs={{0,32},{32,64},{64,96},{96,128},{128,160},{160,192},{192,224},{224... | collective-permute-start | bytes 27656 | tf_op jit(solution)/shard_map/while/body/eval_jaxpr/ppermute | solution.py:18
  253.7 8.0 collective-permute-start.1
  261.7 11.1 %collective-permute-start = (f32[2,1152]{1,0:T(2,128)S(1)}, f32[2,1152]{1,0:T(2,128)S(1)}, u32[]{:S(2)}, u32[]{:S(2)}) collective-permute-start(f32[2,1152]{1,0:T(2,128)S(1)} %copy.20), channel_id=1, source_target_pairs={{0,32},{32,64},{64,96},{96,128},{128,160},{160,192},{192,224},{224... | collective-permute-start | bytes 27656 | tf_op jit(solution)/shard_map/while/body/eval_jaxpr/ppermute | solution.py:18
  264.8 8.0 collective-permute-start.1
  272.8 11.6 %collective-permute-start = (f32[2,1152]{1,0:T(2,128)S(1)}, f32[2,1152]{1,0:T(2,128)S(1)}, u32[]{:S(2)}, u32[]{:S(2)}) collective-permute-start(f32[2,1152]{1,0:T(2,128)S(1)} %copy.20), channel_id=1, source_target_pairs={{0,32},{32,64},{64,96},{96,128},{128,160},{160,192},{192,224},{224... | collective-permute-start | bytes 27656 | tf_op jit(solution)/shard_map/while/body/eval_jaxpr/ppermute | solution.py:18
  276.4 8.0 collective-permute-start.1
  284.4 11.1 %collective-permute-start = (f32[2,1152]{1,0:T(2,128)S(1)}, f32[2,1152]{1,0:T(2,128)S(1)}, u32[]{:S(2)}, u32[]{:S(2)}) collective-permute-start(f32[2,1152]{1,0:T(2,128)S(1)} %copy.20), channel_id=1, source_target_pairs={{0,32},{32,64},{64,96},{96,128},{128,160},{160,192},{192,224},{224... | collective-permute-start | bytes 27656 | tf_op jit(solution)/shard_map/while/body/eval_jaxpr/ppermute | solution.py:18
  287.5 8.0 collective-permute-start.1
  295.5 11.6 %collective-permute-start = (f32[2,1152]{1,0:T(2,128)S(1)}, f32[2,1152]{1,0:T(2,128)S(1)}, u32[]{:S(2)}, u32[]{:S(2)}) collective-permute-start(f32[2,1152]{1,0:T(2,128)S(1)} %copy.20), channel_id=1, source_target_pairs={{0,32},{32,64},{64,96},{96,128},{128,160},{160,192},{192,224},{224... | collective-permute-start | bytes 27656 | tf_op jit(solution)/shard_map/while/body/eval_jaxpr/ppermute | solution.py:18
  299.1 8.0 collective-permute-start.1
  307.1 12.2 %collective-permute-start = (f32[2,1152]{1,0:T(2,128)S(1)}, f32[2,1152]{1,0:T(2,128)S(1)}, u32[]{:S(2)}, u32[]{:S(2)}) collective-permute-start(f32[2,1152]{1,0:T(2,128)S(1)} %copy.20), channel_id=1, source_target_pairs={{0,32},{32,64},{64,96},{96,128},{128,160},{160,192},{192,224},{224... | collective-permute-start | bytes 27656 | tf_op jit(solution)/shard_map/while/body/eval_jaxpr/ppermute | solution.py:18
  311.4 8.0 collective-permute-start.1
  319.4 13.1 %collective-permute-start = (f32[2,1152]{1,0:T(2,128)S(1)}, f32[2,1152]{1,0:T(2,128)S(1)}, u32[]{:S(2)}, u32[]{:S(2)}) collective-permute-start(f32[2,1152]{1,0:T(2,128)S(1)} %copy.20), channel_id=1, source_target_pairs={{0,32},{32,64},{64,96},{96,128},{128,160},{160,192},{192,224},{224... | collective-permute-start | bytes 27656 | tf_op jit(solution)/shard_map/while/body/eval_jaxpr/ppermute | solution.py:18
  324.4 8.0 collective-permute-start.1
  332.5 11.2 %collective-permute-start = (f32[2,1152]{1,0:T(2,128)S(1)}, f32[2,1152]{1,0:T(2,128)S(1)}, u32[]{:S(2)}, u32[]{:S(2)}) collective-permute-start(f32[2,1152]{1,0:T(2,128)S(1)} %copy.20), channel_id=1, source_target_pairs={{0,32},{32,64},{64,96},{96,128},{128,160},{160,192},{192,224},{224... | collective-permute-start | bytes 27656 | tf_op jit(solution)/shard_map/while/body/eval_jaxpr/ppermute | solution.py:18
  335.6 8.0 collective-permute-start.1
  343.6 11.1 %collective-permute-start = (f32[2,1152]{1,0:T(2,128)S(1)}, f32[2,1152]{1,0:T(2,128)S(1)}, u32[]{:S(2)}, u32[]{:S(2)}) collective-permute-start(f32[2,1152]{1,0:T(2,128)S(1)} %copy.20), channel_id=1, source_target_pairs={{0,32},{32,64},{64,96},{96,128},{128,160},{160,192},{192,224},{224... | collective-permute-start | bytes 27656 | tf_op jit(solution)/shard_map/while/body/eval_jaxpr/ppermute | solution.py:18
  346.7 8.0 collective-permute-start.1
  354.7 11.1 %collective-permute-start = (f32[2,1152]{1,0:T(2,128)S(1)}, f32[2,1152]{1,0:T(2,128)S(1)}, u32[]{:S(2)}, u32[]{:S(2)}) collective-permute-start(f32[2,1152]{1,0:T(2,128)S(1)} %copy.20), channel_id=1, source_target_pairs={{0,32},{32,64},{64,96},{96,128},{128,160},{160,192},{192,224},{224... | collective-permute-start | bytes 27656 | tf_op jit(solution)/shard_map/while/body/eval_jaxpr/ppermute | solution.py:18
  357.8 8.0 collective-permute-start.1
  365.8 11.1 %collective-permute-start = (f32[2,1152]{1,0:T(2,128)S(1)}, f32[2,1152]{1,0:T(2,128)S(1)}, u32[]{:S(2)}, u32[]{:S(2)}) collective-permute-start(f32[2,1152]{1,0:T(2,128)S(1)} %copy.20), channel_id=1, source_target_pairs={{0,32},{32,64},{64,96},{96,128},{128,160},{160,192},{192,224},{224... | collective-permute-start | bytes 27656 | tf_op jit(solution)/shard_map/while/body/eval_jaxpr/ppermute | solution.py:18
  368.9 8.0 collective-permute-start.1
  376.9 11.1 %collective-permute-start = (f32[2,1152]{1,0:T(2,128)S(1)}, f32[2,1152]{1,0:T(2,128)S(1)}, u32[]{:S(2)}, u32[]{:S(2)}) collective-permute-start(f32[2,1152]{1,0:T(2,128)S(1)} %copy.20), channel_id=1, source_target_pairs={{0,32},{32,64},{64,96},{96,128},{128,160},{160,192},{192,224},{224... | collective-permute-start | bytes 27656 | tf_op jit(solution)/shard_map/while/body/eval_jaxpr/ppermute | solution.py:18
  380.0 8.0 collective-permute-start.1
  388.0 11.1 %collective-permute-start = (f32[2,1152]{1,0:T(2,128)S(1)}, f32[2,1152]{1,0:T(2,128)S(1)}, u32[]{:S(2)}, u32[]{:S(2)}) collective-permute-start(f32[2,1152]{1,0:T(2,128)S(1)} %copy.20), channel_id=1, source_target_pairs={{0,32},{32,64},{64,96},{96,128},{128,160},{160,192},{192,224},{224... | collective-permute-start | bytes 27656 | tf_op jit(solution)/shard_map/while/body/eval_jaxpr/ppermute | solution.py:18
  391.1 8.0 collective-permute-start.1
  399.1 11.1 %collective-permute-start = (f32[2,1152]{1,0:T(2,128)S(1)}, f32[2,1152]{1,0:T(2,128)S(1)}, u32[]{:S(2)}, u32[]{:S(2)}) collective-permute-start(f32[2,1152]{1,0:T(2,128)S(1)} %copy.20), channel_id=1, source_target_pairs={{0,32},{32,64},{64,96},{96,128},{128,160},{160,192},{192,224},{224... | collective-permute-start | bytes 27656 | tf_op jit(solution)/shard_map/while/body/eval_jaxpr/ppermute | solution.py:18
  402.1 8.0 collective-permute-start.1
  410.2 2.4 copy-start.3
  417.2 1.2 copy-start.6
  421.2 223.5 %all-gather.12.cloned.1.call-start = ((), (), s32[]{:S(2)}) async-start(), calls=%async_computation.6 | async-start | bytes 1253376 | tf_op jit(solution)/shard_map/all_gather | solution.py:11
  559.3 355.3 %all-reduce.52.cloned.1.call-start = ((), (), s32[]{:S(2)}) async-start(), calls=%async_computation.4 | async-start | bytes 344064 | tf_op jit(solution)/shard_map/psum | solution.py:121
Sparse Core Ops, SparseCore 0:
  10.1 74.2 all-gather.5
  86.5 67.7 all-gather.7
  156.5 66.9 all-gather.9
  421.3 137.8 reduce-scatter.1
  562.3 82.3 all-gather.11
  650.1 264.4 all-reduce.51
